TPU v7x, 32 devices: a whole 2x2x4 slice. The times are simulated.
32 devices in a mesh: seq: 8 (over z, y), head: 4 (over x, core).
Axes of the slice: x: 2, y: 2, z: 4, core: 2. Of those that a mesh axis runs over, the one named last changes fastest.
Arguments:
- byte_states: bfloat16 [6144, 1280], P('seq', 'head'), may hold values from -19 to 19
- patch_ids: int32 [6144], P('seq'), may hold values from 0 to 767, never falling along the last dimension, each value on 1 to 16 neighbouring positions
- slot_patch: int32 [768], replicated, may hold values from 0 to 767, each once
- pool_gain: float32 [1280], replicated, may hold values from 0.25 to 1.75
- w_in: bfloat16 [1280, 4096], P('seq', 'head'), may hold values from -0.16910264 to 0.16910264
- attn_gain: float32 [4096], replicated, may hold values from 0.25 to 1.75
- w_qkv: bfloat16 [4096, 3, 1024], P('seq', None, 'head'), may hold values from -0.5105401 to 0.5105401
- w_out: bfloat16 [1024, 4096], P('head'), may hold values from -0.1875 to 0.1875
- w_down: bfloat16 [4096, 1280], P('head', 'seq'), may hold values from -0.34375 to 0.34375
Outputs:
- patch_out: bfloat16 [768, 4096], P('seq', 'head')
- byte_out: bfloat16 [6144, 1280], P('seq', 'head')
Inputs may be any that keep to these rules, and one draw needn't show every extreme that they name: patch_ids never falls along the bytes; each of the 768 patches holds 1 to 16 consecutive bytes, and some patch exactly 16. `slot_patch`: every patch number appears once; slot r belongs to segment r // 96.
All inputs are finite; a program needn't handle non-finite values.
Results may differ from a plain program's by a relative error of at most 0.015.
Values may be sent and summed in bfloat16 or wider, within the bound.
A program may use at most 64 MiB of HBM per device.

v0:
```python
import math

import jax
import jax.numpy as jnp
from jax import lax
from jax.sharding import PartitionSpec as P

HEAD_SIZE = 128
WINDOW = 8


EPSILON = 1e-05
FLOOR_SCORE = -1e30


def rms_scale(values, gain):
    wide = values.astype(jnp.float32)
    return wide * lax.rsqrt(jnp.mean(wide * wide, axis=-1, keepdims=True) + EPSILON) * gain


def over_blocks(carry, keys, labels, update):
    count = labels.shape[0]
    size = math.gcd(count, 512)
    turns = count // size
    key_blocks = jax.tree.map(lambda whole: whole.reshape((turns, size) + whole.shape[1:]), keys)
    label_blocks = labels.reshape(turns, size)

    def advance(state, paired):
        return (update(state, paired[0], paired[1]), None)

    carry, unused = lax.scan(advance, carry, (key_blocks, label_blocks))
    return carry


def softmax_step(carry, scores, allowed, values, equation):
    peak, total, mixed = carry
    scores = jnp.where(allowed, scores, FLOOR_SCORE)
    new_peak = jnp.maximum(peak, jnp.max(scores, axis=-1))
    weights = jnp.where(allowed, jnp.exp(scores - new_peak[..., None]), 0.0)
    rescale = jnp.exp(peak - new_peak)
    total = total * rescale + jnp.sum(weights, axis=-1)
    mixed = mixed * rescale[..., None] + jnp.einsum(
        equation, weights.astype(jnp.bfloat16), values, preferred_element_type=jnp.float32
    )
    return (new_peak, total, mixed)


def body(byte_states, patch_ids, slot_patch, pool_gain, w_in, attn_gain, w_qkv, w_out, w_down):
    rows_each = slot_patch.shape[0] // lax.axis_size("seq")
    bytes_here = byte_states.shape[0]
    cross_size = byte_states.shape[1]
    match = (slot_patch[:, None] == patch_ids[None, :]).astype(jnp.bfloat16)
    pooled = lax.psum_scatter(
        jnp.dot(match, byte_states, preferred_element_type=jnp.float32),
        "seq",
        scatter_dimension=0,
        tiled=True,
    ).astype(jnp.bfloat16)
    pooled_full = lax.all_gather(pooled, "head", axis=1, tiled=True)
    normed = rms_scale(pooled_full, pool_gain).astype(jnp.bfloat16)
    columns = normed
    embed = jnp.dot(
        columns, lax.all_gather(w_in, "seq", axis=0, tiled=True), preferred_element_type=jnp.float32
    ).astype(jnp.bfloat16)
    embed_full = lax.all_gather(embed, "head", axis=1, tiled=True)
    attn_in = rms_scale(embed_full, attn_gain).astype(jnp.bfloat16)
    heads_here = w_qkv.shape[2] // HEAD_SIZE
    piece = lax.all_gather(w_qkv, "seq", axis=0, tiled=True)
    columns = attn_in
    projected = jnp.dot(
        columns, piece.reshape(piece.shape[0], -1), preferred_element_type=jnp.float32
    ).astype(jnp.bfloat16)
    projected = projected.reshape(rows_each, 3, heads_here, HEAD_SIZE)
    queries = projected[:, 0].transpose(1, 0, 2)
    keys_here = projected[:, 1]
    values_here = projected[:, 2]
    own_labels = lax.dynamic_slice_in_dim(slot_patch, lax.axis_index("seq") * rows_each, rows_each)
    head_scale = 1.0 / math.sqrt(HEAD_SIZE)

    def attend_keys(carry, pieces):

        def update(state, block, block_labels):
            key_block, value_block = block
            scores = (
                jnp.einsum("hqd,khd->hqk", queries, key_block, preferred_element_type=jnp.float32)
                * head_scale
            )
            allowed = block_labels[None, None, :] <= own_labels[None, :, None]
            return softmax_step(state, scores, allowed, value_block, "hqk,khd->hqd")

        return over_blocks(carry, pieces, slot_patch, update)

    attn_init = (
        jnp.full((heads_here, rows_each), FLOOR_SCORE, jnp.float32),
        jnp.zeros((heads_here, rows_each), jnp.float32),
        jnp.zeros((heads_here, rows_each, HEAD_SIZE), jnp.float32),
    )
    peak, total, mixed = attend_keys(
        attn_init,
        (
            lax.all_gather(keys_here, "seq", axis=0, tiled=True),
            lax.all_gather(values_here, "seq", axis=0, tiled=True),
        ),
    )
    attended = (
        (mixed / total[..., None])
        .astype(jnp.bfloat16)
        .transpose(1, 0, 2)
        .reshape(rows_each, heads_here * HEAD_SIZE)
    )
    columns_out = lax.all_to_all(w_out, "head", split_axis=1, concat_axis=0, tiled=True)
    added = jnp.dot(
        lax.all_gather(attended, "head", axis=1, tiled=True),
        columns_out,
        preferred_element_type=jnp.float32,
    )
    stream = (embed.astype(jnp.float32) + added).astype(jnp.bfloat16)
    down_part = jnp.dot(
        stream,
        lax.all_gather(w_down, "seq", axis=1, tiled=True),
        preferred_element_type=jnp.float32,
    )
    patch_states = lax.psum_scatter(down_part, "head", scatter_dimension=1, tiled=True).astype(
        jnp.bfloat16
    )
    cross_scale = 1.0 / math.sqrt(cross_size)

    def attend_patches(carry, piece):

        def update(state, block, block_labels):
            scores = (
                jnp.einsum("bc,kc->bk", byte_states, block, preferred_element_type=jnp.float32)
                * cross_scale
            )
            allowed = (block_labels[None, :] <= patch_ids[:, None]) & (
                block_labels[None, :] > patch_ids[:, None] - WINDOW
            )
            return softmax_step(state, scores, allowed, block, "bk,kc->bc")

        return over_blocks(carry, piece, slot_patch, update)

    cross_init = (
        jnp.full((bytes_here,), FLOOR_SCORE, jnp.float32),
        jnp.zeros((bytes_here,), jnp.float32),
        jnp.zeros((bytes_here, cross_size), jnp.float32),
    )
    cross_peak, cross_total, cross_mixed = attend_patches(
        cross_init, lax.all_gather(patch_states, "seq", axis=0, tiled=True)
    )
    reached = cross_mixed / cross_total[:, None]
    byte_out = (byte_states.astype(jnp.float32) + reached).astype(jnp.bfloat16)
    return (stream, byte_out)


def solution(mesh):
    placed = (
        P("seq", "head"),
        P("seq"),
        P(),
        P(),
        P("seq", "head"),
        P(),
        P("seq", None, "head"),
        P("head", None),
        P("head", "seq"),
    )
    return jax.shard_map(
        body,
        mesh=mesh,
        in_specs=placed,
        out_specs=(P("seq", "head"), P("seq", "head")),
        check_vma=False,
    )
```

profile of v0, /device:TPU:1, one launch (start us, length us, event | category | flops | bytes accessed | tf_op | source)
XLA Modules:
  0.0 374.6 jit_solution(10534478967150290168)
XLA Ops:
  7.2 0.0 reduce-scatter.5.cloned.1.call-start
  7.2 3.0 fusion.35
  10.2 0.0 reduce-scatter.5.cloned.1.call-update
  10.2 0.0 all-gather.7.cloned.1.call-start
  10.2 0.7 all-gather.7.cloned.1.call-update
  11.0 0.0 all-gather.9.cloned.1.call-start
  11.0 1.2 copy.31
  12.2 0.0 all-gather.9.cloned.1.call-update
  12.2 2.5 copy.38
  14.7 4.4 %all-to-all-start = ((bf16[256,4,1024]{0,2,1:T(8,128)(2,1)}), bf16[256,4,1024]{0,2,1:T(8,128)(2,1)S(1)}, u32[]{:S(2)}, u32[]{:S(2)}) async-start(bf16[256,4,1024]{0,2,1:T(8,128)(2,1)} %bitcast.83), calls=%async_computation.1 | async-start | bytes 4194304 | tf_op jit(solution)/shard_map/all_to_all | solution.py:111
  19.1 0.6 all-gather.11.cloned.1.call-update
  19.7 0.0 reduce-scatter.7.cloned.1.call-start
  19.8 0.1 dynamic_slice.29
  19.9 23.9 %all-to-all-done = bf16[256,4,1024]{0,2,1:T(8,128)(2,1)S(1)} async-done(((bf16[256,4,1024]{0,2,1:T(8,128)(2,1)}), bf16[256,4,1024]{0,2,1:T(8,128)(2,1)S(1)}, u32[]{:S(2)}, u32[]{:S(2)}) %all-to-all-start) | async-done | bytes 2097184 | tf_op jit(solution)/shard_map/all_to_all | solution.py:111
  43.7 1.4 copy-done
  45.1 3.0 copy.39
  48.2 27.7 %reduce-scatter.5.cloned.1.call-done = f32[96,320]{1,0:T(8,128)} async-done(((f32[768,320]{1,0:T(8,128)}), f32[96,320]{1,0:T(8,128)}) %reduce-scatter.5.cloned.1.call-update) | async-done | bytes 122896 | tf_op jit(solution)/shard_map/reduce_scatter | solution.py:53
  75.8 0.9 convert_bitcast_fusion
  76.8 8.0 %all-gather.2 = bf16[4,320,96]{1,2,0:T(8,128)(2,1)S(1)} all-gather(bf16[1,320,96]{1,2,0:T(8,128)(2,1)S(1)} %convert_bitcast_fusion), channel_id=1, replica_groups=mesh['seq'=8,'head'=4] {'head'}, dimensions={0}, use_global_device_ids=true | all-gather | bytes 307200 | tf_op jit(solution)/shard_map/all_gather | solution.py:59
  84.8 0.2 copy.30
  84.9 0.4 reshape.109
  85.3 0.1 multiply_reduce_fusion
  85.4 46.6 %all-gather.7.cloned.1.call-done = bf16[1280,1024]{1,0:T(8,128)(2,1)} async-done(((bf16[160,1024]{1,0:T(8,128)(2,1)}), bf16[1280,1024]{1,0:T(8,128)(2,1)}) %all-gather.7.cloned.1.call-update) | async-done | bytes 2621456 | tf_op jit(solution)/shard_map/all_gather | solution.py:63
  132.0 2.3 convolution_convert_fusion
  134.4 10.3 %all_gather.29 = bf16[96,4096]{1,0:T(8,128)(2,1)S(1)} all-gather(bf16[96,1024]{1,0:T(8,128)(2,1)S(1)} %convolution_convert_fusion), channel_id=1, replica_groups=mesh['seq'=8,'head'=4] {'head'}, dimensions={1}, use_global_device_ids=true | all-gather | bytes 983040 | tf_op jit(solution)/shard_map/all_gather | solution.py:65
  144.7 0.3 fusion.37
  145.0 88.4 %all-gather.9.cloned.1.call-done = bf16[4096,3,256]{0,2,1:T(8,128)(2,1)} async-done(((bf16[512,3,256]{0,2,1:T(8,128)(2,1)}), bf16[4096,3,256]{0,2,1:T(8,128)(2,1)}) %all-gather.9.cloned.1.call-update) | async-done | bytes 6291472 | tf_op jit(solution)/shard_map/all_gather | solution.py:68
  233.4 4.9 %convolution_convert_fusion.1 = bf16[96,768]{1,0:T(8,128)(2,1)S(1)} fusion(bf16[4096,768]{0,1:T(8,128)(2,1)} %bitcast.84, bf16[96,4096]{1,0:T(8,128)(2,1)S(1)} %all_gather.29, f32[4096]{0:T(1024)S(1)} %copy-done.6, f32[96]{0:T(128)S(1)} %add_rsqrt_fusion), kind=kOutput, calls=%fused_computation.65 | convolution fusion | flops 605626368 | bytes 7242112 | tf_op jit(solution)/shard_map/dot_general | solution.py:70
  238.4 0.1 fusion.51
  238.5 25.5 %all-gather = bf16[768,1,2,128]{3,0,2,1:T(8,128)(2,1)S(1)} all-gather(bf16[96,1,2,128]{3,0,2,1:T(8,128)(2,1)S(1)} %copy.44), channel_id=2, replica_groups=mesh['seq'=8,'head'=4] {'seq'}, dimensions={0}, use_global_device_ids=true | all-gather | bytes 442368 | tf_op jit(solution)/shard_map/all_gather | solution.py:101
  264.0 26.0 %all-gather.1 = bf16[768,1,2,128]{3,0,2,1:T(8,128)(2,1)S(1)} all-gather(bf16[96,1,2,128]{3,0,2,1:T(8,128)(2,1)S(1)} %copy.46), channel_id=3, replica_groups=mesh['seq'=8,'head'=4] {'seq'}, dimensions={0}, use_global_device_ids=true | all-gather | bytes 442368 | tf_op jit(solution)/shard_map/all_gather | solution.py:102
  290.0 2.7 while.32
  290.0 0.1 broadcast_compare_fusion.2
  290.1 0.3 fusion.78
  290.4 0.2 fusion.80
  290.6 0.2 convolution_add_fusion.5
  290.9 0.1 broadcast_compare_fusion.2
  291.0 0.3 fusion.78
  291.3 0.2 fusion.80
  291.5 0.2 convolution_add_fusion.5
  291.8 0.1 broadcast_compare_fusion.2
  291.9 0.3 fusion.78
  292.2 0.2 fusion.80
  292.4 0.2 convolution_add_fusion.5
  292.7 0.1 copy_bitcast_fusion
  292.8 19.0 %all_gather.33 = bf16[96,1024]{1,0:T(8,128)(2,1)S(1)} all-gather(bf16[96,256]{1,0:T(8,128)(2,1)S(1)} %copy_bitcast_fusion), channel_id=1, replica_groups=mesh['seq'=8,'head'=4] {'head'}, dimensions={1}, use_global_device_ids=true | all-gather | bytes 245760 | tf_op jit(solution)/shard_map/all_gather | solution.py:113
  311.8 0.5 fusion.42
  312.3 0.0 all-gather.11.cloned.1.call-done
  312.3 3.5 convolution_bitcast_fusion
  315.9 0.0 reduce-scatter.7.cloned.1.call-update
  315.9 20.1 %reduce-scatter.7.cloned.1.call-done = f32[320,96]{1,0:T(8,128)} async-done(((f32[1280,96]{1,0:T(8,128)}), f32[320,96]{1,0:T(8,128)}) %reduce-scatter.7.cloned.1.call-update) | async-done | bytes 122896
  336.0 1.0 copy.41
  337.1 26.0 %all_gather.35 = bf16[768,320]{1,0:T(8,128)(2,1)S(1)} all-gather(bf16[96,320]{1,0:T(8,128)(2,1)S(1)} %copy.41), channel_id=1, replica_groups=mesh['seq'=8,'head'=4] {'seq'}, dimensions={0}, use_global_device_ids=true | all-gather | bytes 552960 | tf_op jit(solution)/shard_map/all_gather | solution.py:148
  363.1 4.0 %while.33 = (s32[]{:T(128)}, f32[768]{0:T(1024)S(1)}, f32[768]{0:T(1024)S(1)}, f32[768,320]{0,1:T(8,128)S(1)}, s32[3,256]{1,0:T(4,128)S(1)}, /*index=5*/s32[768]...) while((s32[]{:T(128)}, f32[768]{0:T(1024)S(1)}, ...), condition=%wide.region_11.12_spmd.clone, body=%wide.region_8.11_spmd.clone.sunk | while | flops 255939072 | bytes 5295229 | solution.py:31
  363.1 0.4 fusion.85
  363.5 0.2 fusion.86
  363.8 0.6 convolution_add_fusion.6
  364.4 0.4 fusion.85
  364.9 0.2 fusion.86
  365.1 0.6 convolution_add_fusion.6
  365.8 0.4 fusion.85
  366.2 0.2 fusion.86
  366.5 0.6 convolution_add_fusion.6
  367.1 0.9 add_convert_fusion
  (58 shorter events, 0.3 us)
Async XLA Ops:
  7.2 3.8 %copy-start.3 = (bf16[512,3,256]{2,0,1:T(8,128)(2,1)S(1)}, bf16[512,3,256]{2,0,1:T(8,128)(2,1)}, u32[]{:S(2)}) copy-start(bf16[512,3,256]{2,0,1:T(8,128)(2,1)} %param.19) | copy-start | bytes 2359300
  7.2 68.7 %reduce-scatter.5.cloned.1.call-start = ((), (), s32[]{:S(2)}) async-start(), calls=%async_computation.3 | async-start | bytes 1327104 | tf_op jit(solution)/shard_map/reduce_scatter | solution.py:53
  10.2 2.0 copy-start.1
  10.2 121.8 %all-gather.7.cloned.1.call-start = ((), (), s32[]{:S(2)}) async-start(), calls=%async_computation.4 | async-start | bytes 2949120 | tf_op jit(solution)/shard_map/all_gather | solution.py:63
  11.0 222.5 %all-gather.9.cloned.1.call-start = ((), (), s32[]{:S(2)}) async-start(), calls=%async_computation.5 | async-start | bytes 7077888 | tf_op jit(solution)/shard_map/all_gather | solution.py:68
  14.7 5.0 %copy-start.8 = (s32[768]{0:T(1024)S(1)}, s32[768]{0:T(1024)}, u32[]{:S(2)}) copy-start(s32[768]{0:T(1024)} %param.15) | copy-start | bytes 9220
  14.7 29.0 %all-to-all-start = ((bf16[256,4,1024]{0,2,1:T(8,128)(2,1)}), bf16[256,4,1024]{0,2,1:T(8,128)(2,1)S(1)}, u32[]{:S(2)}, u32[]{:S(2)}) async-start(bf16[256,4,1024]{0,2,1:T(8,128)(2,1)} %bitcast.83), calls=%async_computation.1 | async-start | bytes 4194304 | tf_op jit(solution)/shard_map/all_to_all | solution.py:111
  19.1 293.2 %all-gather.11.cloned.1.call-start = ((), (), s32[]{:S(2)}) async-start(), calls=%async_computation.6 | async-start | bytes 2949120 | tf_op jit(solution)/shard_map/all_gather | solution.py:120
  19.7 316.4 %reduce-scatter.7.cloned.1.call-start = ((), (), s32[]{:S(2)}) async-start(), calls=%async_computation.7 | async-start | bytes 819200
  43.7 1.4 copy-start
  48.1 83.9 %copy-start.7 = (f32[1280]{0:T(1024)S(1)}, f32[1280]{0:T(1024)}, u32[]{:S(2)}) copy-start(f32[1280]{0:T(1024)} %param.16) | copy-start | bytes 15364
  85.4 148.0 %copy-start.6 = (f32[4096]{0:T(1024)S(1)}, f32[4096]{0:T(1024)}, u32[]{:S(2)}) copy-start(f32[4096]{0:T(1024)} %param.18) | copy-start | bytes 49156
  312.3 24.8 %copy-start.4 = (bf16[96,1024]{1,0:T(8,128)(2,1)}, bf16[96,1024]{1,0:T(8,128)(2,1)S(1)}, u32[]{:S(2)}) copy-start(bf16[96,1024]{1,0:T(8,128)(2,1)S(1)} %fusion.42) | copy-start | bytes 589828
  312.3 50.8 %copy-start.2 = (s32[768]{0:T(1024)S(1)}, s32[768]{0:T(1024)}, u32[]{:S(2)}) copy-start(s32[768]{0:T(1024)} %param.14) | copy-start | bytes 9220
  312.3 50.8 %copy-start.5 = (bf16[768,320]{0,1:T(8,128)(2,1)S(1)}, bf16[768,320]{0,1:T(8,128)(2,1)}, u32[]{:S(2)}) copy-start(bf16[768,320]{0,1:T(8,128)(2,1)} %param.13) | copy-start | bytes 1474564
Sparse Core Ops, SparseCore 0:
  11.4 64.4 reduce-scatter.4
  78.0 53.9 all-gather.6
  134.1 99.3 all-gather.8
  235.5 59.5 all-gather.10
  316.0 19.9 reduce-scatter.6
where the time goes:
time: 381 us; the launch traced here: 375 us
  waiting for transfers between devices  208 us (55%)
  blocking collectives  115 us (30%)
  matrix products  18.7 us (5%)
  between operations  14 us (4%)
  local copies, waits for them, and re-layouts  10 us (3%)
  starting transfers between devices  4.55 us (1%)
  other arithmetic  4.02 us (1%)
    all_gather x1, waiting for transfers between devices, body(): piece = lax.all_gather(w_qkv, 'seq', axis=0, tiled=True)  88.4 us
    all_gather x1, waiting for transfers between devices, body(): lax.all_gather(w_in, 'seq', axis=0, tiled=True)  46.6 us
    reduce_scatter x1, waiting for transfers between devices, body(): lax.psum_scatter(jnp.dot(match, byte_states, preferred_element_type=jnp.f...  27.7 us
    all_gather x1, blocking collectives, body(): lax.all_gather(values_here, 'seq', axis=0, tiled=True)  26 us
    all_gather x1, blocking collectives, body(): lax.all_gather(patch_states, 'seq', axis=0, tiled=True)  26 us
    all_gather x1, blocking collectives, body(): lax.all_gather(keys_here, 'seq', axis=0, tiled=True)  25.5 us
    all_to_all x1, waiting for transfers between devices, body(): lax.all_to_all(w_out, 'head', split_axis=1, concat_axis=0, tiled=True)  23.9 us
    unnamed x6, waiting for transfers between devices  21.4 us
  transfers between devices with their start and end apart: 6, of which 5 were waited for; matrix products, arithmetic and copies ran while one was open for 5% of the time, Pallas kernels for 0%

commit v1 on v0

v1 whole, which is shorter than its diff:
```python
import functools
import math

import jax
import jax.numpy as jnp
from jax import lax
from jax.experimental import pallas as pl
from jax.experimental.pallas import tpu as pltpu
from jax.sharding import PartitionSpec as P

HEAD_SIZE = 128
WINDOW = 8
EPSILON = 1e-05
FLOOR_SCORE = -1e30
MESH = pl.DeviceIdType.MESH
F32 = jnp.float32
BF16 = jnp.bfloat16


def dot(a, b):
    return lax.dot_general(a, b, (((1,), (0,)), ((), ())), preferred_element_type=F32)


def dot_t(a, b):
    return lax.dot_general(a, b, (((1,), (1,)), ((), ())), preferred_element_type=F32)


def merge_rows(block):
    r, m, n = block.shape
    if m % 16 and r > 1:
        return block.astype(F32).reshape(r * m, n).astype(block.dtype)
    return block.reshape(r * m, n)


class SeqGather:
    def __init__(self, n_seq, src, buf, sems):
        self.n_z = n_seq // 2
        self.src, self.buf = src, buf
        self.send_z, self.send_y, self.recv, self.own = sems
        self.me = lax.axis_index("seq")
        self.z, self.y = self.me // 2, lax.rem(self.me, 2)
        self.pending = []

    def slot(self, z, y):
        return z * 2 + y

    def copy(self, src, slot, target, send_sem):
        return pltpu.make_async_remote_copy(
            src_ref=src,
            dst_ref=self.buf.at[slot],
            send_sem=send_sem,
            recv_sem=self.recv.at[slot],
            device_id={"seq": target},
            device_id_type=MESH,
        )

    def start(self):
        self.local = pltpu.make_async_copy(self.src, self.buf.at[self.me], self.own.at[0])
        self.local.start()
        c = self.copy(self.src, self.me, self.slot(self.z, 1 - self.y), self.send_y.at[0])
        c.start()
        self.pending.append(c)
        for dz in range(1, self.n_z):
            to = lax.rem(self.z + dz, self.n_z)
            c = self.copy(self.src, self.me, self.slot(to, self.y), self.send_z.at[dz])
            c.start()
            self.pending.append(c)

    def forward(self, dz):
        z = lax.rem(self.z + self.n_z - dz, self.n_z)
        slot = self.slot(z, self.y)
        c = self.copy(
            self.buf.at[slot], slot, self.slot(self.z, 1 - self.y), self.send_y.at[dz]
        )
        c.wait_recv()
        c.start()
        self.pending.append(c)

    def forward_all(self):
        for dz in range(1, self.n_z):
            self.forward(dz)

    def finish(self):
        self.local.wait()
        for z in range(self.n_z):
            slot = self.slot(z, 1 - self.y)
            self.copy(self.buf.at[slot], slot, self.me, self.send_y.at[0]).wait_recv()

    def drain(self):
        for c in self.pending:
            c.wait_send()


class HeadExchange:
    def __init__(self, n_head, buf, send, recv):
        self.n = n_head
        self.buf, self.send, self.recv = buf, send, recv
        self.me = lax.axis_index("head")
        self.pending = []

    def start(self, src_of):
        for d in range(1, self.n):
            to = lax.rem(self.me + d, self.n)
            c = pltpu.make_async_remote_copy(
                src_ref=src_of(to),
                dst_ref=self.buf.at[self.me],
                send_sem=self.send.at[d],
                recv_sem=self.recv.at[self.me],
                device_id={"head": to},
                device_id_type=MESH,
            )
            c.start()
            self.pending.append(c)

    def finish(self):
        for d in range(1, self.n):
            src = lax.rem(self.me + d, self.n)
            pltpu.make_async_remote_copy(
                src_ref=self.buf.at[src],
                dst_ref=self.buf.at[src],
                send_sem=self.send.at[d],
                recv_sem=self.recv.at[src],
                device_id={"head": src},
                device_id_type=MESH,
            ).wait_recv()

    def drain(self):
        for c in self.pending:
            c.wait_send()


def kernel(
    n_seq, n_head,
    x_ref, idr_ref, idc_ref, slotc_ref, slotr_ref, pg_ref, ag_ref,
    w_in_ref, w_qkv_ref, w_out_ref, w_down_ref,
    patch_out_ref, byte_out_ref,
    g_in, g_qkv, g_down, g_kv, g_ps, wo_g, part, rs_buf, pool_g, emb_g, att_g,
    kv_src, ps_src, down_src, down_g,
    gz, gy, gr, go, hs, hr, rss, rsr, wos,
):
    me, mh = lax.axis_index("seq"), lax.axis_index("head")
    rows = patch_out_ref.shape[0]
    width = patch_out_ref.shape[1]
    n_bytes, cross = x_ref.shape
    ratio = n_seq // n_head

    barrier = pltpu.get_barrier_semaphore()
    for d in range(1, n_seq):
        pl.semaphore_signal(
            barrier, inc=1, device_id={"seq": lax.rem(me + d, n_seq)}, device_id_type=MESH
        )
    for d in range(1, n_head):
        pl.semaphore_signal(
            barrier, inc=1, device_id={"head": lax.rem(mh + d, n_head)}, device_id_type=MESH
        )
    pl.semaphore_wait(barrier, n_seq + n_head - 2)

    def gather(i, src, buf):
        return SeqGather(n_seq, src, buf, (gz.at[i], gy.at[i], gr.at[i], go.at[i]))

    def exchange(i, buf):
        return HeadExchange(n_head, buf, hs.at[i], hr.at[i])

    in_gather = gather(0, w_in_ref, g_in)
    qkv_gather = gather(1, w_qkv_ref, g_qkv)
    down_gather = gather(2, w_down_ref, g_down)
    kv_gather = gather(3, kv_src, g_kv)
    ps_gather = gather(4, ps_src, g_ps)
    wo_x, pool_x, emb_x, att_x, down_x = (
        exchange(i, buf) for i, buf in enumerate((wo_g, pool_g, emb_g, att_g, down_g))
    )

    in_gather.start()

    def rs_copy(d):
        to = lax.rem(me + d, n_seq)
        return pltpu.make_async_remote_copy(
            src_ref=part.at[to],
            dst_ref=rs_buf.at[me],
            send_sem=rss.at[d],
            recv_sem=rsr.at[me],
            device_id={"seq": to},
            device_id_type=MESH,
        )

    def pool(to):
        match = jnp.where(slotc_ref[to] == idr_ref[...], 1.0, 0.0).astype(BF16)
        return dot(match, x_ref[...])

    def pool_step(d, carry):
        to = lax.rem(me + d, n_seq)
        part[to] = pool(to).astype(BF16)
        rs_copy(d).start()
        return carry

    lax.fori_loop(1, n_seq, pool_step, 0)
    qkv_gather.start()
    wo_x.start(lambda to: w_out_ref.at[:, pl.ds(pl.multiple_of(to * width, 128), width)])
    wo_own = pltpu.make_async_copy(
        w_out_ref.at[:, pl.ds(pl.multiple_of(mh * width, 128), width)], wo_g.at[mh], wos.at[0]
    )
    wo_own.start()
    pooled = pool(me)
    in_gather.forward_all()
    for d in range(1, n_seq):
        src = lax.rem(me + d, n_seq)
        pltpu.make_async_remote_copy(
            src_ref=rs_buf.at[src],
            dst_ref=rs_buf.at[src],
            send_sem=rss.at[d],
            recv_sem=rsr.at[src],
            device_id={"seq": src},
            device_id_type=MESH,
        ).wait_recv()
        pooled = pooled + rs_buf[src].astype(F32)
    pool_g[mh] = pooled.astype(BF16)
    pool_x.start(lambda to: pool_g.at[mh])
    pool_x.finish()

    def square_sum(buf):
        total = jnp.zeros((rows, 1), F32)
        for i in range(n_head):
            block = buf[i].astype(F32)
            total = total + jnp.sum(block * block, axis=-1, keepdims=True)
        return total

    scale = lax.rsqrt(square_sum(pool_g) / (cross * n_head) + EPSILON)
    in_gather.finish()
    embed = jnp.zeros((rows, width), F32)
    for i in range(n_head):
        normed = (pool_g[i].astype(F32) * scale * pg_ref[i]).astype(BF16)
        embed = embed + dot(normed, merge_rows(g_in[i * ratio : (i + 1) * ratio]))
    emb_g[mh] = embed.astype(BF16)
    emb_x.start(lambda to: emb_g.at[mh])
    qkv_gather.forward_all()
    down_gather.start()
    emb_x.finish()
    scale = lax.rsqrt(square_sum(emb_g) / (width * n_head) + EPSILON)
    qkv_gather.finish()
    projected = jnp.zeros((rows, w_qkv_ref.shape[1]), F32)
    for i in range(n_head):
        attn_in = (emb_g[i].astype(F32) * scale * ag_ref[i]).astype(BF16)
        projected = projected + dot(attn_in, merge_rows(g_qkv[i * ratio : (i + 1) * ratio]))
    projected = projected.astype(BF16)
    third = projected.shape[1] // 3
    kv_src[...] = projected[:, third:]
    kv_gather.start()
    queries = projected[:, :third]
    kv_gather.forward_all()
    down_gather.forward_all()
    kv_gather.finish()

    own = slotc_ref[me]
    allowed = slotr_ref[...] <= own
    for j in range(third // HEAD_SIZE):
        cols = slice(j * HEAD_SIZE, (j + 1) * HEAD_SIZE)
        keys = merge_rows(g_kv[:, :, j * HEAD_SIZE : (j + 1) * HEAD_SIZE])
        values = merge_rows(g_kv[:, :, third + j * HEAD_SIZE : third + (j + 1) * HEAD_SIZE])
        scores = dot_t(queries[:, cols], keys) * (1.0 / math.sqrt(HEAD_SIZE))
        scores = jnp.where(allowed, scores, FLOOR_SCORE)
        peak = jnp.max(scores, axis=-1, keepdims=True)
        weights = jnp.where(allowed, jnp.exp(scores - peak), 0.0)
        total = jnp.sum(weights, axis=-1, keepdims=True)
        att_g[mh, :, cols] = (dot(weights.astype(BF16), values) / total).astype(BF16)
    att_x.start(lambda to: att_g.at[mh])
    wo_own.wait()
    wo_x.finish()
    att_x.finish()
    added = jnp.zeros((rows, width), F32)
    for i in range(n_head):
        added = added + dot(att_g[i], wo_g[i])
    stream = (emb_g[mh].astype(F32) + added).astype(BF16)
    patch_out_ref[...] = stream

    down_gather.finish()
    for i in range(n_head):
        down_src[i] = dot_t(stream, merge_rows(g_down[i * ratio : (i + 1) * ratio]))
    down_x.start(lambda to: down_src.at[to])
    down_x.finish()
    states = down_src[mh]
    for d in range(1, n_head):
        states = states + down_g[lax.rem(mh + d, n_head)]
    ps_src[...] = states.astype(BF16)
    ps_gather.start()
    ps_gather.forward_all()
    ps_gather.finish()

    size = math.gcd(n_bytes, 256)

    def cross_step(t, carry):
        at = pl.ds(pl.multiple_of(t * size, size), size)
        block = x_ref[at, :]
        states = merge_rows(g_ps[...])
        ids = idc_ref[at, :]
        allowed = (slotr_ref[...] <= ids) & (slotr_ref[...] > ids - WINDOW)
        scores = dot_t(block, states) * (1.0 / math.sqrt(cross))
        scores = jnp.where(allowed, scores, FLOOR_SCORE)
        peak = jnp.max(scores, axis=-1, keepdims=True)
        weights = jnp.where(allowed, jnp.exp(scores - peak), 0.0)
        total = jnp.sum(weights, axis=-1, keepdims=True)
        mixed = dot(weights.astype(BF16), states) / total
        byte_out_ref[at, :] = (block.astype(F32) + mixed).astype(BF16)
        return carry

    lax.fori_loop(0, n_bytes // size, cross_step, 0)

    for g in (in_gather, qkv_gather, down_gather, kv_gather, ps_gather):
        g.drain()
    for x in (wo_x, pool_x, emb_x, att_x, down_x):
        x.drain()
    for d in range(1, n_seq):
        rs_copy(d).wait_send()


def body(byte_states, patch_ids, slot_patch, pool_gain, w_in, attn_gain, w_qkv, w_out, w_down):
    n_seq, n_head = lax.axis_size("seq"), lax.axis_size("head")
    rows = slot_patch.shape[0] // n_seq
    n_bytes, cross = byte_states.shape
    width = w_in.shape[1]
    qkv = w_qkv.reshape(w_qkv.shape[0], -1)
    third = w_qkv.shape[2]
    down = w_down.T
    n_z = n_seq // 2
    vmem = pl.BlockSpec(memory_space=pltpu.VMEM)
    anywhere = pl.BlockSpec(memory_space=pl.ANY)
    dma = pltpu.SemaphoreType.DMA
    return pl.pallas_call(
        functools.partial(kernel, n_seq, n_head),
        out_shape=(
            jax.ShapeDtypeStruct((rows, width), BF16),
            jax.ShapeDtypeStruct((n_bytes, cross), BF16),
        ),
        in_specs=[vmem] * 7 + [anywhere] * 4,
        out_specs=(vmem, vmem),
        scratch_shapes=[
            pltpu.VMEM((n_seq,) + w_in.shape, BF16),
            pltpu.VMEM((n_seq,) + qkv.shape, BF16),
            pltpu.VMEM((n_seq,) + down.shape, BF16),
            pltpu.VMEM((n_seq, rows, 2 * third), BF16),
            pltpu.VMEM((n_seq, rows, cross), BF16),
            pltpu.VMEM((n_head, w_out.shape[0], width), BF16),
            pltpu.VMEM((n_seq, rows, cross), BF16),
            pltpu.VMEM((n_seq, rows, cross), BF16),
            pltpu.VMEM((n_head, rows, cross), BF16),
            pltpu.VMEM((n_head, rows, width), BF16),
            pltpu.VMEM((n_head, rows, third), BF16),
            pltpu.VMEM((rows, 2 * third), BF16),
            pltpu.VMEM((rows, cross), BF16),
            pltpu.VMEM((n_head, rows, cross), F32),
            pltpu.VMEM((n_head, rows, cross), F32),
            dma((5, n_z)),
            dma((5, n_z)),
            dma((5, n_seq)),
            dma((5, 1)),
            dma((5, n_head)),
            dma((5, n_head)),
            dma((n_seq,)),
            dma((n_seq,)),
            dma((1,)),
        ],
        compiler_params=pltpu.CompilerParams(
            collective_id=0, has_side_effects=True, vmem_limit_bytes=56 * 1024 * 1024
        ),
    )(
        byte_states,
        patch_ids.reshape(1, -1),
        patch_ids.reshape(-1, 1),
        slot_patch.reshape(n_seq, rows, 1),
        slot_patch.reshape(1, -1),
        pool_gain.reshape(n_head, 1, cross),
        attn_gain.reshape(n_head, 1, width),
        w_in,
        qkv,
        w_out,
        down,
    )


def solution(mesh):
    placed = (
        P("seq", "head"),
        P("seq"),
        P(),
        P(),
        P("seq", "head"),
        P(),
        P("seq", None, "head"),
        P("head", None),
        P("head", "seq"),
    )
    return jax.shard_map(
        body,
        mesh=mesh,
        in_specs=placed,
        out_specs=(P("seq", "head"), P("seq", "head")),
        check_vma=False,
    )
```

time: 381 us -> 240 us (0.63); the launches traced: 375 us -> 240 us
  Pallas kernels: 0 us -> 225 us
  waiting for transfers between devices: 208 us -> 0 us
  blocking collectives: 115 us -> 0 us
  matrix products: 18.7 us -> 0 us
  between operations: 14 us -> 0.66 us
  starting transfers between devices: 4.55 us -> 0 us
  local copies, waits for them, and re-layouts: 10 us -> 14.5 us
  other arithmetic: 4.02 us -> 0 us
    pallas_call x0 -> x1, Pallas kernels: none -> 225 us  [body(): pl.pallas_call(functools.partial(kernel, n_seq, n_head), out_shape=(jax.S...]
    all_gather x3 -> x0, waiting for transfers between devices: 135 us -> none  [the longest x1 88.4 us: body(): piece = lax.all_gather(w_qkv, 'seq', axis=0, tiled=True)]
    all_gather x6 -> x0, blocking collectives: 115 us -> none  [the longest x1 26 us: body(): lax.all_gather(values_here, 'seq', axis=0, tiled=True)]
    reduce_scatter x1 -> x0, waiting for transfers between devices: 27.7 us -> none  [body(): lax.psum_scatter(jnp.dot(match, byte_states, preferred_element_type=jnp.f...]
    all_to_all x1 -> x0, waiting for transfers between devices: 23.9 us -> none  [body(): lax.all_to_all(w_out, 'head', split_axis=1, concat_axis=0, tiled=True)]
    unnamed x6 -> x0, waiting for transfers between devices: 21.4 us -> none
    dot_general x16 -> x0, matrix products: 15.2 us -> none  [the longest x1 4.88 us: body(): jnp.dot(columns, piece.reshape(piece.shape[0], -1), preferred_element_typ...]
    reshape x2 -> x6, local copies, waits for them, and re-layouts: 0.05 us -> 8.48 us  [the longest x1 1.74 us: body(): slot_patch.reshape(n_seq, rows, 1)]
  transfers between devices with their start and end apart: 6 -> 0, of which waited for: 5 -> 0; matrix products, arithmetic and copies ran while one was open for 5% -> 0% of each run, Pallas kernels for 0% -> 0%
where the time goes in v1:
time: 240 us
  Pallas kernels  225 us (94%)
  local copies, waits for them, and re-layouts  14.5 us (6%)
    pallas_call x1, Pallas kernels, body(): pl.pallas_call(functools.partial(kernel, n_seq, n_head), out_shape=(jax.S...  225 us

profile of v1, /device:TPU:1, one launch (start us, length us, event | category | flops | bytes accessed | tf_op | source)
XLA Modules:
  0.0 239.8 jit_solution(1208839884927241608)
XLA Ops:
  0.6 0.0 copy-start
  0.6 1.3 reshape.25.idr_ref
  2.0 1.3 reshape.28.slotr_ref
  3.3 1.4 reshape.29.pg_ref
  4.6 1.6 reshape.32.idc_ref
  6.2 1.7 reshape.33.slotc_ref
  8.0 2.1 copy.15.x_ref
  10.0 0.0 copy-done
  10.0 0.3 copy.14
  10.3 1.2 copy.18.w_qkv_ref
  11.5 224.7 %shard_map.104 = (bf16[96,1024]{1,0:T(8,128)(2,1)}, bf16[768,320]{1,0:T(8,128)(2,1)}) custom-call(bf16[768,320]{1,0:T(8,128)(2,1)} %copy.15.x_ref, s32[1,768]{1,0:T(1,128)} %reshape.25.idr_ref, s32[768,1]{1,0:T(8,128)} %reshape.32.idc_ref, s32[8,96,1]{2,1,0:T(8,128)} %reshape.33.slotc_ref, s32[1,768]{1,0:T(1,128)} %reshape.28.slotr_ref, ...), custom_call_target="tpu_custom_call" | custom-call | tf_op jit(solution)/shard_map/pallas_call | solution.py:327
  236.2 2.1 copy.19
  238.2 1.6 copy.21
Async XLA Ops:
  0.6 9.4 %copy-start = (bf16[512,3,256]{2,0,1:T(8,128)(2,1)S(1)}, bf16[512,3,256]{2,0,1:T(8,128)(2,1)}, u32[]{:S(2)}) copy-start(bf16[512,3,256]{2,0,1:T(8,128)(2,1)} %param.15) | copy-start | bytes 2359300

commit v2 on v1

v2 whole, which is shorter than its diff:
```python
import functools
import math

import jax
import jax.numpy as jnp
from jax import lax
from jax.experimental import pallas as pl
from jax.experimental.pallas import tpu as pltpu
from jax.sharding import PartitionSpec as P

HEAD_SIZE = 128
WINDOW = 8
EPSILON = 1e-05
FLOOR_SCORE = -1e30
MESH = pl.DeviceIdType.MESH
F32 = jnp.float32
BF16 = jnp.bfloat16


def dot(a, b):
    return lax.dot_general(a, b, (((1,), (0,)), ((), ())), preferred_element_type=F32)


def dot_t(a, b):
    return lax.dot_general(a, b, (((1,), (1,)), ((), ())), preferred_element_type=F32)


def lanes(n):
    return -(-n // 128) * 128


def merge_rows(block):
    r, m, n = block.shape
    if m % 16 and r > 1:
        return block.astype(F32).reshape(r * m, n).astype(block.dtype)
    return block.reshape(r * m, n)


class Gather:
    def __init__(self, axis, src, buf, sems):
        self.axis = axis
        self.n_z = lax.axis_size(axis) // 2
        self.src, self.buf = src, buf
        self.send_z, self.send_y, self.recv, self.own = sems
        self.me = lax.axis_index(axis)
        self.z, self.y = self.me // 2, lax.rem(self.me, 2)
        self.pending = []

    def slot(self, z, y):
        return z * 2 + y

    def copy(self, src, slot, target, send_sem):
        return pltpu.make_async_remote_copy(
            src_ref=src,
            dst_ref=self.buf.at[slot],
            send_sem=send_sem,
            recv_sem=self.recv.at[slot],
            device_id={self.axis: target},
            device_id_type=MESH,
        )

    def start(self):
        self.local = pltpu.make_async_copy(self.src, self.buf.at[self.me], self.own.at[0])
        self.local.start()
        for dz in range(1, self.n_z):
            to = lax.rem(self.z + dz, self.n_z)
            c = self.copy(self.src, self.me, self.slot(to, self.y), self.send_z.at[dz])
            c.start()
            self.pending.append(c)
        c = self.copy(self.src, self.me, self.slot(self.z, 1 - self.y), self.send_y.at[0])
        c.start()
        self.pending.append(c)

    def forward_all(self):
        for dz in range(1, self.n_z):
            z = lax.rem(self.z + self.n_z - dz, self.n_z)
            slot = self.slot(z, self.y)
            c = self.copy(
                self.buf.at[slot], slot, self.slot(self.z, 1 - self.y), self.send_y.at[dz]
            )
            c.wait_recv()
            c.start()
            self.pending.append(c)

    def finish(self):
        self.local.wait()
        for z in range(self.n_z):
            slot = self.slot(z, 1 - self.y)
            self.copy(self.buf.at[slot], slot, self.me, self.send_y.at[0]).wait_recv()

    def drain(self):
        for c in self.pending:
            c.wait_send()


class Exchange:
    def __init__(self, n, me, device, buf, send, recv):
        self.n, self.me, self.device = n, me, device
        self.buf, self.send, self.recv = buf, send, recv
        self.pending = []

    def send_to(self, src, d):
        to = lax.rem(self.me + d, self.n)
        c = pltpu.make_async_remote_copy(
            src_ref=src,
            dst_ref=self.buf.at[self.me],
            send_sem=self.send.at[d],
            recv_sem=self.recv.at[self.me],
            device_id=self.device(to),
            device_id_type=MESH,
        )
        c.start()
        self.pending.append(c)

    def start(self, src_of):
        for d in range(1, self.n):
            self.send_to(src_of(lax.rem(self.me + d, self.n)), d)

    def wait_from(self, src, d):
        pltpu.make_async_remote_copy(
            src_ref=self.buf.at[src],
            dst_ref=self.buf.at[src],
            send_sem=self.send.at[d],
            recv_sem=self.recv.at[src],
            device_id=self.device(src),
            device_id_type=MESH,
        ).wait_recv()

    def finish(self):
        for d in range(1, self.n):
            self.wait_from(lax.rem(self.me + d, self.n), d)

    def drain(self):
        for c in self.pending:
            c.wait_send()


def kernel(
    n_seq, n_head,
    x_ref, small_ref, ag_ref,
    w_in_ref, w_qkv_ref, w_out_ref, w_down_ref,
    patch_out_ref, byte_out_ref,
    g_in, g_qkv, g_down, g_kv, g_ps, wo_g, part, rs_buf, pool_g, emb_g, att_g,
    kv_src, ps_src, down_src, down_g, slotc_ref, pool_src, emb_src, att_src,
    a_src, a_buf, prj_src, prj_buf,
    gz, gy, gr, go, jz, jy, jr, jo, hs, hr, zs, zr, rss, rsr, wos, qs,
):
    me, mh = lax.axis_index("seq"), lax.axis_index("head")
    rows = patch_out_ref.shape[0]
    width = patch_out_ref.shape[1]
    cross, n_bytes = x_ref.shape
    n_z = n_seq // 2
    z, y = me // 2, lax.rem(me, 2)
    n_patches = n_seq * rows
    third = w_qkv_ref.shape[2]
    ratio = n_seq // n_head

    barrier = pltpu.get_barrier_semaphore()
    for d in range(1, n_seq):
        pl.semaphore_signal(
            barrier, inc=1, device_id={"seq": lax.rem(me + d, n_seq)}, device_id_type=MESH
        )
    for d in range(1, n_head):
        pl.semaphore_signal(
            barrier, inc=1, device_id={"head": lax.rem(mh + d, n_head)}, device_id_type=MESH
        )
    pl.semaphore_wait(barrier, n_seq + n_head - 2)

    def gather(i, src, buf):
        return Gather("seq", src, buf, (gz.at[i], gy.at[i], gr.at[i], go.at[i]))

    def head_gather(i, src, buf):
        return Gather("head", src, buf, (jz.at[i], jy.at[i], jr.at[i], jo.at[i]))

    def exchange(i, buf):
        return Exchange(n_head, mh, lambda to: {"head": to}, buf, hs.at[i], hr.at[i])

    def z_exchange(i, buf):
        return Exchange(n_z, z, lambda to: {"seq": to * 2 + y}, buf, zs.at[i], zr.at[i])

    in_gather = gather(0, w_in_ref, g_in)
    down_gather = gather(1, w_down_ref, g_down)
    kv_gather = gather(2, kv_src, g_kv)
    ps_gather = gather(3, ps_src, g_ps)
    pool_x = head_gather(0, pool_src, pool_g)
    emb_x = head_gather(1, emb_src, emb_g)
    att_x = head_gather(2, att_src, att_g)
    wo_x, down_x = exchange(0, wo_g), exchange(1, down_g)
    a_x, prj_x = z_exchange(0, a_buf), z_exchange(1, prj_buf)
    ids = small_ref[:, :n_bytes]
    slotr = small_ref[:, n_bytes : n_bytes + n_patches]

    in_gather.start()
    wo_x.start(lambda to: w_out_ref.at[:, pl.ds(pl.multiple_of(to * width, 128), width)])
    wo_own = pltpu.make_async_copy(
        w_out_ref.at[:, pl.ds(pl.multiple_of(mh * width, 128), width)], wo_g.at[mh], wos.at[0]
    )
    wo_own.start()
    qkv_own = pltpu.make_async_copy(w_qkv_ref, g_qkv.at[y], qs.at[0])
    qkv_own.start()

    down = lax.broadcasted_iota(jnp.int32, (rows, n_patches), 0)
    along = lax.broadcasted_iota(jnp.int32, (rows, n_patches), 1)

    def slot_step(i, carry):
        slotc_ref[i] = jnp.sum(
            jnp.where(down + i * rows == along, slotr, 0.0), axis=-1, keepdims=True
        )
        return carry

    lax.fori_loop(0, n_seq, slot_step, 0)

    def rs_copy(d):
        to = lax.rem(me + d, n_seq)
        return pltpu.make_async_remote_copy(
            src_ref=part.at[to],
            dst_ref=rs_buf.at[me],
            send_sem=rss.at[d],
            recv_sem=rsr.at[me],
            device_id={"seq": to},
            device_id_type=MESH,
        )

    def pool(to):
        match = jnp.where(slotc_ref[to] == ids, 1.0, 0.0).astype(BF16)
        return dot_t(match, x_ref[...])

    def pool_step(d, carry):
        to = lax.rem(me + d, n_seq)
        part[to] = pool(to).astype(BF16)
        rs_copy(d).start()
        return carry

    lax.fori_loop(1, n_seq, pool_step, 0)
    pooled = pool(me)
    in_gather.forward_all()
    qkv_copy = pltpu.make_async_remote_copy(
        src_ref=w_qkv_ref,
        dst_ref=g_qkv.at[y],
        send_sem=qs.at[1],
        recv_sem=qs.at[2],
        device_id={"seq": z * 2 + 1 - y},
        device_id_type=MESH,
    )
    qkv_copy.start()
    for d in range(1, n_seq):
        src = lax.rem(me + d, n_seq)
        pltpu.make_async_remote_copy(
            src_ref=rs_buf.at[src],
            dst_ref=rs_buf.at[src],
            send_sem=rss.at[d],
            recv_sem=rsr.at[src],
            device_id={"seq": src},
            device_id_type=MESH,
        ).wait_recv()
        pooled = pooled + rs_buf[src].astype(F32)
    pool_src[...] = pooled.astype(BF16)
    pool_x.start()
    pool_x.forward_all()
    pool_x.finish()
    down_gather.start()

    def square_sum(buf):
        total = jnp.zeros((rows, 1), F32)
        for i in range(n_head):
            block = buf[i].astype(F32)
            total = total + jnp.sum(block * block, axis=-1, keepdims=True)
        return total

    scale = lax.rsqrt(square_sum(pool_g) / (cross * n_head) + EPSILON)
    in_gather.finish()
    embed = jnp.zeros((rows, width), F32)
    for i in range(n_head):
        at = n_bytes + n_patches + i * lanes(cross)
        gain = small_ref[:, at : at + cross]
        normed = (pool_g[i].astype(F32) * scale * gain).astype(BF16)
        embed = embed + dot(normed, merge_rows(g_in[i * ratio : (i + 1) * ratio]))
    emb_src[...] = embed.astype(BF16)
    emb_x.start()
    emb_x.forward_all()
    emb_x.finish()
    scale = lax.rsqrt(square_sum(emb_g) / (width * n_head) + EPSILON)
    for d in list(range(1, n_z)) + [0]:
        to = lax.rem(z + d, n_z)
        a_src[to] = (emb_g[to].astype(F32) * scale * ag_ref[to]).astype(BF16)
        if d:
            a_x.send_to(a_src.at[to], d)

    def project(block):
        return [dot(block, merge_rows(g_qkv[:, j])) for j in range(3)]

    qkv_own.wait()
    qkv_copy.wait_recv()
    projected = project(a_src[z])
    down_gather.forward_all()
    for d in range(n_z - 1, 0, -1):
        source = lax.rem(z + d, n_z)
        a_x.wait_from(source, d)
        for j, piece in enumerate(project(a_buf[source])):
            prj_src[source, :, j * third : (j + 1) * third] = piece.astype(BF16)
        prj_x.send_to(prj_src.at[source], d)
    prj_x.finish()
    for d in range(1, n_z):
        source = lax.rem(z + d, n_z)
        projected = [
            piece + prj_buf[source, :, j * third : (j + 1) * third].astype(F32)
            for j, piece in enumerate(projected)
        ]
    queries = projected[0].astype(BF16)
    kv_src[:, :third] = projected[1].astype(BF16)
    kv_src[:, third:] = projected[2].astype(BF16)
    kv_gather.start()
    kv_gather.forward_all()
    kv_gather.finish()

    own = slotc_ref[me]
    allowed = slotr <= own
    for j in range(third // HEAD_SIZE):
        cols = slice(j * HEAD_SIZE, (j + 1) * HEAD_SIZE)
        keys = merge_rows(g_kv[:, :, j * HEAD_SIZE : (j + 1) * HEAD_SIZE])
        values = merge_rows(g_kv[:, :, third + j * HEAD_SIZE : third + (j + 1) * HEAD_SIZE])
        scores = dot_t(queries[:, cols], keys) * (1.0 / math.sqrt(HEAD_SIZE))
        scores = jnp.where(allowed, scores, FLOOR_SCORE)
        peak = jnp.max(scores, axis=-1, keepdims=True)
        weights = jnp.where(allowed, jnp.exp(scores - peak), 0.0)
        total = jnp.sum(weights, axis=-1, keepdims=True)
        att_src[:, cols] = (dot(weights.astype(BF16), values) / total).astype(BF16)
    att_x.start()
    att_x.forward_all()
    wo_own.wait()
    wo_x.finish()
    att_x.finish()
    added = jnp.zeros((rows, width), F32)
    for i in range(n_head):
        added = added + dot(att_g[i], wo_g[i])
    stream = (emb_src[...].astype(F32) + added).astype(BF16)
    patch_out_ref[...] = stream

    down_gather.finish()

    def down_part(i):
        pieces = [dot_t(stream, g_down[i * ratio + j]) for j in range(ratio)]
        return pieces[0] if ratio == 1 else jnp.concatenate(pieces, axis=-1)

    for d in range(1, n_head):
        to = lax.rem(mh + d, n_head)
        down_src[to] = down_part(to).astype(BF16)
        down_x.send_to(down_src.at[to], d)
    states = down_part(mh)
    down_x.finish()
    for d in range(1, n_head):
        states = states + down_g[lax.rem(mh + d, n_head)].astype(F32)
    ps_src[...] = states.astype(BF16)
    ps_gather.start()
    ps_gather.forward_all()
    ps_gather.finish()

    size = math.gcd(n_bytes, 256)

    slots = slotc_ref[...].reshape(n_patches, 1)

    def cross_step(t, carry):
        at = pl.ds(pl.multiple_of(t * size, 128), size)
        block = x_ref[:, at]
        states = merge_rows(g_ps[...])
        labels = small_ref[:, at]
        allowed = (slots <= labels) & (slots > labels - WINDOW)
        scores = dot(states, block) * (1.0 / math.sqrt(cross))
        scores = jnp.where(allowed, scores, FLOOR_SCORE)
        peak = jnp.max(scores, axis=0, keepdims=True)
        weights = jnp.where(allowed, jnp.exp(scores - peak), 0.0)
        total = jnp.sum(weights, axis=0, keepdims=True)
        mixed = lax.dot_general(
            states, weights.astype(BF16), (((0,), (0,)), ((), ())), preferred_element_type=F32
        )
        byte_out_ref[:, at] = (block.astype(F32) + mixed / total).astype(BF16)
        return carry

    lax.fori_loop(0, n_bytes // size, cross_step, 0)

    qkv_copy.wait_send()
    for g in (in_gather, down_gather, kv_gather, ps_gather, pool_x, emb_x, att_x):
        g.drain()
    for x in (wo_x, down_x, a_x, prj_x):
        x.drain()
    for d in range(1, n_seq):
        rs_copy(d).wait_send()


def body(byte_states, patch_ids, slot_patch, pool_gain, w_in, attn_gain, w_qkv, w_out, w_down):
    n_seq, n_head = lax.axis_size("seq"), lax.axis_size("head")
    rows = slot_patch.shape[0] // n_seq
    n_bytes, cross = byte_states.shape
    width = w_in.shape[1]
    qkv = w_qkv.transpose(1, 0, 2)
    third = w_qkv.shape[2]
    down = w_down.T
    n_z = n_seq // 2
    gains = jnp.pad(
        pool_gain.reshape(n_head, cross), ((0, 0), (0, lanes(cross) - cross))
    ).reshape(-1)
    small = jnp.concatenate([patch_ids.astype(F32), slot_patch.astype(F32), gains])
    small = jnp.pad(small, (0, -small.shape[0] % 1024)).reshape(1, -1)
    vmem = pl.BlockSpec(memory_space=pltpu.VMEM)
    anywhere = pl.BlockSpec(memory_space=pl.ANY)
    dma = pltpu.SemaphoreType.DMA
    n_x = n_head // 2
    stream, byte_out = pl.pallas_call(
        functools.partial(kernel, n_seq, n_head),
        out_shape=(
            jax.ShapeDtypeStruct((rows, width), BF16),
            jax.ShapeDtypeStruct((cross, n_bytes), BF16),
        ),
        in_specs=[vmem] * 3 + [anywhere] * 4,
        out_specs=(vmem, vmem),
        scratch_shapes=[
            pltpu.VMEM((n_seq,) + w_in.shape, BF16),
            pltpu.VMEM((2,) + qkv.shape, BF16),
            pltpu.VMEM((n_seq,) + down.shape, BF16),
            pltpu.VMEM((n_seq, rows, 2 * third), BF16),
            pltpu.VMEM((n_seq, rows, cross), BF16),
            pltpu.VMEM((n_head, w_out.shape[0], width), BF16),
            pltpu.VMEM((n_seq, rows, cross), BF16),
            pltpu.VMEM((n_seq, rows, cross), BF16),
            pltpu.VMEM((n_head, rows, cross), BF16),
            pltpu.VMEM((n_head, rows, width), BF16),
            pltpu.VMEM((n_head, rows, third), BF16),
            pltpu.VMEM((rows, 2 * third), BF16),
            pltpu.VMEM((rows, cross), BF16),
            pltpu.VMEM((n_head, rows, cross), BF16),
            pltpu.VMEM((n_head, rows, cross), BF16),
            pltpu.VMEM((n_seq, rows, 1), F32),
            pltpu.VMEM((rows, cross), BF16),
            pltpu.VMEM((rows, width), BF16),
            pltpu.VMEM((rows, third), BF16),
            pltpu.VMEM((n_z, rows, width), BF16),
            pltpu.VMEM((n_z, rows, width), BF16),
            pltpu.VMEM((n_z, rows, 3 * third), BF16),
            pltpu.VMEM((n_z, rows, 3 * third), BF16),
            dma((4, n_z)),
            dma((4, n_z)),
            dma((4, n_seq)),
            dma((4, 1)),
            dma((3, n_x)),
            dma((3, n_x)),
            dma((3, n_head)),
            dma((3, 1)),
            dma((2, n_head)),
            dma((2, n_head)),
            dma((2, n_z)),
            dma((2, n_z)),
            dma((n_seq,)),
            dma((n_seq,)),
            dma((1,)),
            dma((3,)),
        ],
        compiler_params=pltpu.CompilerParams(
            collective_id=0, has_side_effects=True, vmem_limit_bytes=56 * 1024 * 1024
        ),
    )(
        byte_states.T,
        small,
        attn_gain.reshape(n_head, 1, width),
        w_in,
        qkv,
        w_out,
        down,
    )
    return stream, byte_out.T


def solution(mesh):
    placed = (
        P("seq", "head"),
        P("seq"),
        P(),
        P(),
        P("seq", "head"),
        P(),
        P("seq", None, "head"),
        P("head", None),
        P("head", "seq"),
    )
    return jax.shard_map(
        body,
        mesh=mesh,
        in_specs=placed,
        out_specs=(P("seq", "head"), P("seq", "head")),
        check_vma=False,
    )
```

time: 240 us -> 169 us (0.70)
  Pallas kernels: 225 us -> 162 us
  local copies, waits for them, and re-layouts: 14.5 us -> 4.25 us
    pallas_call x1, Pallas kernels: 225 us -> 162 us  [body(): pl.pallas_call(functools.partial(kernel, n_seq, n_head), out_shape=(jax.S...]
    reshape x6 -> x2, local copies, waits for them, and re-layouts: 8.48 us -> 0.78 us  [the longest x1 0.77 us: body(): pool_gain.reshape(n_head, cross)]
where the time goes in v2:
time: 169 us
  Pallas kernels  162 us (96%)
  local copies, waits for them, and re-layouts  4.25 us (3%)
  other arithmetic  1.99 us (1%)
    pallas_call x1, Pallas kernels, body(): pl.pallas_call(functools.partial(kernel, n_seq, n_head), out_shape=(jax.S...  162 us
    unnamed x2, local copies, waits for them, and re-layouts  3.46 us

profile of v2, /device:TPU:1, one launch (start us, length us, event | category | flops | bytes accessed | tf_op | source)
XLA Modules:
  0.0 168.5 jit_solution(1687423779887584576)
XLA Ops:
  0.6 0.7 convert_element_type.8
  1.3 0.7 convert_element_type.9
  2.0 0.8 reshape.16
  2.8 0.6 pad_maximum_fusion
  3.4 161.6 %shard_map.104 = (bf16[96,1024]{1,0:T(8,128)(2,1)}, bf16[320,768]{1,0:T(8,128)(2,1)}) custom-call(bf16[320,768]{1,0:T(8,128)(2,1)} %bitcast.7, f32[1,3072]{1,0:T(1,128)} %bitcast.10, f32[4,1,1024]{2,1,0:T(1,128)} %bitcast.11, bf16[160,1024]{1,0:T(8,128)(2,1)} %w_in_ref.1, bf16[3,512,256]{2,1,0:T(8,128)(2,1)} %bitcast.6, bf16[256,4096]{1,0:T(8,128)(2,1)} %w_out_ref.1, ...), custom_call_target="tpu_custom_call" | custom-call | tf_op jit(solution)/shard_map/pallas_call | solution.py:408
  165.0 1.6 copy.13
  166.7 1.8 %copy.14 = bf16[768,320]{0,1:T(8,128)(2,1)} copy(bf16[768,320]{0,1:T(8,128)(2,1)} %bitcast.8) | data formatting | bytes 983040
  (2 shorter events, 0.0 us)

commit v3 on v2

--- a/solution.py
+++ b/solution.py
@@ -143,14 +143,14 @@
     g_in, g_qkv, g_down, g_kv, g_ps, wo_g, part, rs_buf, pool_g, emb_g, att_g,
     kv_src, ps_src, down_src, down_g, slotc_ref, pool_src, emb_src, att_src,
     a_src, a_buf, prj_src, prj_buf,
-    gz, gy, gr, go, jz, jy, jr, jo, hs, hr, zs, zr, rss, rsr, wos, qs,
+    gz, gy, gr, go, jz, jy, jr, jo, hs, hr, zs, zr, rss, rsr, wos, qs, shs,
 ):
     me, mh = lax.axis_index("seq"), lax.axis_index("head")
     rows = patch_out_ref.shape[0]
     width = patch_out_ref.shape[1]
     cross, n_bytes = x_ref.shape
     n_z = n_seq // 2
-    z, y = me // 2, lax.rem(me, 2)
+    z, y, core = me // 2, lax.rem(me, 2), lax.rem(mh, 2)
     n_patches = n_seq * rows
     third = w_qkv_ref.shape[2]
     ratio = n_seq // n_head
@@ -243,6 +243,7 @@
         device_id_type=MESH,
     )
     qkv_copy.start()
+    down_gather.start()
     for d in range(1, n_seq):
         src = lax.rem(me + d, n_seq)
         pltpu.make_async_remote_copy(
@@ -258,7 +259,6 @@
     pool_x.start()
     pool_x.forward_all()
     pool_x.finish()
-    down_gather.start()
 
     def square_sum(buf):
         total = jnp.zeros((rows, 1), F32)
@@ -284,7 +284,20 @@
         to = lax.rem(z + d, n_z)
         a_src[to] = (emb_g[to].astype(F32) * scale * ag_ref[to]).astype(BF16)
         if d:
-            a_x.send_to(a_src.at[to], d)
+
+            @pl.when(core == d % 2)
+            def send(to=to, d=d):
+                a_x.send_to(a_src.at[to], d)
+
+    def share(source, d):
+        return pltpu.make_async_remote_copy(
+            src_ref=a_buf.at[source],
+            dst_ref=a_buf.at[source],
+            send_sem=shs.at[d],
+            recv_sem=zr.at[0, source],
+            device_id={"head": mh + 1 - 2 * core},
+            device_id_type=MESH,
+        )
 
     def project(block):
         return [dot(block, merge_rows(g_qkv[:, j])) for j in range(3)]
@@ -293,12 +306,17 @@
     qkv_copy.wait_recv()
     projected = project(a_src[z])
     down_gather.forward_all()
-    for d in range(n_z - 1, 0, -1):
-        source = lax.rem(z + d, n_z)
+    for d in range(1, n_z):
+        source = lax.rem(z + n_z - d, n_z)
         a_x.wait_from(source, d)
+
+        @pl.when(core == d % 2)
+        def pass_on(source=source, d=d):
+            share(source, d).start()
+
         for j, piece in enumerate(project(a_buf[source])):
             prj_src[source, :, j * third : (j + 1) * third] = piece.astype(BF16)
-        prj_x.send_to(prj_src.at[source], d)
+        prj_x.send_to(prj_src.at[source], n_z - d)
     prj_x.finish()
     for d in range(1, n_z):
         source = lax.rem(z + d, n_z)
@@ -381,7 +399,22 @@
     qkv_copy.wait_send()
     for g in (in_gather, down_gather, kv_gather, ps_gather, pool_x, emb_x, att_x):
         g.drain()
-    for x in (wo_x, down_x, a_x, prj_x):
+    for d in range(1, n_z):
+        source = lax.rem(z + n_z - d, n_z)
+
+        @pl.when(core == d % 2)
+        def settle(source=source, d=d):
+            share(source, d).wait_send()
+            pltpu.make_async_remote_copy(
+                src_ref=a_src.at[source],
+                dst_ref=a_buf.at[source],
+                send_sem=zs.at[0, d],
+                recv_sem=zr.at[0, source],
+                device_id={"seq": source * 2 + y},
+                device_id_type=MESH,
+            ).wait_send()
+
+    for x in (wo_x, down_x, prj_x):
         x.drain()
     for d in range(1, n_seq):
         rs_copy(d).wait_send()
@@ -453,6 +486,7 @@
             dma((n_seq,)),
             dma((1,)),
             dma((3,)),
+            dma((n_z,)),
         ],
         compiler_params=pltpu.CompilerParams(
             collective_id=0, has_side_effects=True, vmem_limit_bytes=56 * 1024 * 1024

time: 169 us -> 151 us (0.89)
  Pallas kernels: 162 us -> 144 us
    pallas_call x1, Pallas kernels: 162 us -> 144 us  [body(): pl.pallas_call(functools.partial(kernel, n_seq, n_head), out_shape=(jax.S...]
where the time goes in v3:
time: 151 us; the launch traced here: 150 us
  Pallas kernels  144 us (95%)
  local copies, waits for them, and re-layouts  4.25 us (3%)
  other arithmetic  1.99 us (1%)
    pallas_call x1, Pallas kernels, body(): pl.pallas_call(functools.partial(kernel, n_seq, n_head), out_shape=(jax.S...  144 us
    unnamed x2, local copies, waits for them, and re-layouts  3.46 us

profile of v3, /device:TPU:1, one launch (start us, length us, event | category | flops | bytes accessed | tf_op | source)
XLA Modules:
  0.0 150.4 jit_solution(15774813274329007182)
XLA Ops:
  0.6 0.7 convert_element_type.8
  1.3 0.7 convert_element_type.9
  2.0 0.8 reshape.16
  2.8 0.6 pad_maximum_fusion
  3.4 143.6 %shard_map.104 = (bf16[96,1024]{1,0:T(8,128)(2,1)}, bf16[320,768]{1,0:T(8,128)(2,1)}) custom-call(bf16[320,768]{1,0:T(8,128)(2,1)} %bitcast.7, f32[1,3072]{1,0:T(1,128)} %bitcast.10, f32[4,1,1024]{2,1,0:T(1,128)} %bitcast.11, bf16[160,1024]{1,0:T(8,128)(2,1)} %w_in_ref.1, bf16[3,512,256]{2,1,0:T(8,128)(2,1)} %bitcast.6, bf16[256,4096]{1,0:T(8,128)(2,1)} %w_out_ref.1, ...), custom_call_target="tpu_custom_call" | custom-call | tf_op jit(solution)/shard_map/pallas_call | solution.py:441
  147.0 1.6 %copy.13 = bf16[96,1024]{1,0:T(8,128)(2,1)} copy(bf16[96,1024]{1,0:T(8,128)(2,1)} %get-tuple-element.8) | data formatting | bytes 393216
  148.6 1.8 %copy.14 = bf16[768,320]{0,1:T(8,128)(2,1)} copy(bf16[768,320]{0,1:T(8,128)(2,1)} %bitcast.8) | data formatting | bytes 983040
  (2 shorter events, 0.0 us)
